TPU v7x, 512 devices: a whole 4x8x8 slice. The times are simulated.
512 devices in a mesh: geo: 128 (over z, y, core), rep: 4 (over x).
Axes of the slice: x: 4, y: 8, z: 8, core: 2. Of those that a mesh axis runs over, the one named last changes fastest.
Arguments:
- base: float32 [1048576], P(('geo', 'rep')), may hold values from 0.5 to 2
- job_res: int32 [1048576], P(('geo', 'rep')), may hold values from 0 to 255
- job_slot: int32 [1048576], P(('geo', 'rep')), may hold values from 0 to 4095
- job_cell: int32 [1048576], P(('geo', 'rep')), may hold values from 0 to 29
- needed: int32 [128, 128, 1], P('geo'), may hold values from 0 to 7
- lam_res: float32 [30, 32768], P(None, 'geo'), may hold values from -2 to 2
- lam_work: float32 [30, 32768], P(None, 'geo'), may hold values from -2 to 2
- target_res: float32 [30, 32768], P(None, 'geo'), may hold values from 0.3 to 3
- target_work: float32 [30, 32768], P(None, 'geo'), may hold values from 0.3 to 3
Outputs:
- step_res: float32 [30, 32768], P(None, 'geo')
- step_work: float32 [30, 32768], P(None, 'geo')
- resid_res: float32 [30, 32768], P(None, 'geo')
- resid_work: float32 [30, 32768], P(None, 'geo')
Inputs may be any that keep to these rules, and one draw needn't show every extreme that they name: needed[g, p, k] is a block of owner p's tracts; block b covers that owner's local tracts b * 32 to b * 32 + 31.
All inputs are finite; a program needn't handle non-finite values.
Results may differ from a plain program's by a relative error of at most 0.0003.
Values sent between devices are 32-bit elements; how exact they have to be, the bound alone decides.
A program may use at most 64 MiB of HBM per device.

v0:
```python
import jax
import jax.numpy as jnp
from jax import lax
from jax.sharding import PartitionSpec as P

BLK = 32
ITERS = 3


RIDGE = 0.5


def body(base, job_res, job_slot, job_cell, needed, lam_res, lam_work, target_res, target_work):
    cells, tracts_dev = lam_res.shape
    blocks_dev = tracts_dev // BLK
    requests = lax.all_to_all(needed[0], "geo", split_axis=0, concat_axis=0, tiled=True)
    sources, listed = requests.shape
    onehot = (
        requests[:, :, None] == jnp.arange(blocks_dev, dtype=jnp.int32)[None, None, :]
    ).astype(jnp.float32)
    slot_shape = (sources, listed, cells, BLK)
    slot_count = sources * listed * cells * BLK
    res_index = job_cell * tracts_dev + job_res
    work_index = (job_slot // BLK * cells + job_cell) * BLK + job_slot % BLK

    def serve(table):
        blocks = table.reshape(cells, blocks_dev, BLK).transpose(1, 0, 2)
        return jnp.take(blocks, requests, axis=0)

    def pick(fetched):
        return fetched.reshape(-1)[work_index]

    def fold(arrived):
        return jnp.einsum("skb,skcx->cbx", onehot, arrived, precision=lax.Precision.HIGHEST)

    def totals(values):
        res_part = jax.ops.segment_sum(values, res_index, num_segments=cells * tracts_dev).reshape(
            cells, tracts_dev
        )
        work_part = jax.ops.segment_sum(values, work_index, num_segments=slot_count).reshape(
            slot_shape
        )
        arrived = lax.all_to_all(work_part, "geo", split_axis=0, concat_axis=0, tiled=True)
        folded = fold(arrived)
        return lax.psum((res_part, folded.reshape(cells, tracts_dev)), "rep")

    def squares(part_res, part_work):
        local = jnp.sum(part_res * part_res) + jnp.sum(part_work * part_work)
        return lax.psum(local, "geo")

    fetched_lam = lax.all_to_all(serve(lam_work), "geo", split_axis=0, concat_axis=0, tiled=True)
    weight = base * jnp.exp(lam_res.reshape(-1)[res_index] + pick(fetched_lam))
    total_res, total_work = totals(weight)
    resid_res = -(total_res - target_res)
    resid_work = -(total_work - target_work)
    step_res = jnp.zeros_like(resid_res)
    step_work = jnp.zeros_like(resid_work)
    dir_res, dir_work = (resid_res, resid_work)
    norm_now = squares(resid_res, resid_work)
    for turn in range(ITERS):
        served = serve(dir_work)
        dir_piece = lax.all_to_all(served, "geo", split_axis=0, concat_axis=0, tiled=True)
        along = dir_res.reshape(-1)[res_index] + pick(dir_piece)
        image_res, image_work = totals(weight * along)
        image_res = image_res + RIDGE * dir_res
        image_work = image_work + RIDGE * dir_work
        local_curv = jnp.sum(dir_res * image_res) + jnp.sum(dir_work * image_work)
        alpha = norm_now / lax.psum(local_curv, "geo")
        step_res = step_res + alpha * dir_res
        step_work = step_work + alpha * dir_work
        resid_res = resid_res - alpha * image_res
        resid_work = resid_work - alpha * image_work
        norm_next = squares(resid_res, resid_work)
        dir_res = resid_res + norm_next / norm_now * dir_res
        dir_work = resid_work + norm_next / norm_now * dir_work
        norm_now = norm_next
    return (step_res, step_work, resid_res, resid_work)


def solution(mesh):
    in_specs = (
        P(("geo", "rep")),
        P(("geo", "rep")),
        P(("geo", "rep")),
        P(("geo", "rep")),
        P("geo", None, None),
        P(None, "geo"),
        P(None, "geo"),
        P(None, "geo"),
        P(None, "geo"),
    )
    out_specs = (P(None, "geo"), P(None, "geo"), P(None, "geo"), P(None, "geo"))
    return jax.shard_map(body, mesh=mesh, in_specs=in_specs, out_specs=out_specs, check_vma=False)
```

profile of v0, /device:TPU:1, one launch (start us, length us, event | category | flops | bytes accessed | tf_op | source)
XLA Modules:
  0.0 1842.4 jit_solution(11171462655316426278)
XLA Ops:
  2.0 18.4 all-to-all-start
  21.3 10.5 all-to-all-done
  54.3 11.8 gather_fusion
  66.1 8.8 all-to-all-done.1
  87.7 11.8 gather_fusion.1
  99.6 11.6 scatter_custom_fusion.1
  129.8 11.7 scatter_custom_fusion
  141.5 8.9 all-to-all-done.2
  156.9 14.2 all-reduce.4
  185.2 9.0 all-to-all-start.3
  194.2 11.8 gather_fusion.2
  227.5 11.8 gather_fusion.3
  239.3 11.8 scatter_custom_fusion.3
  271.0 11.4 scatter_custom_fusion.2
  296.8 11.5 all-reduce.3
  310.8 249.6 %all-reduce = (f32[]{:T(128)}, f32[]{:T(128)}) all-reduce(f32[]{:T(128)S(6)} %add.157, f32[]{:T(128)S(6)} %add.161), channel_id=1, replica_groups=mesh['geo'=128,'rep'=4] {'geo'}, use_global_device_ids=true, to_apply=%region_6.8 | all-reduce | flops 2 | bytes 16 | tf_op jit(solution)/shard_map/psum | solution.py:49
  564.3 247.3 %psum.104 = f32[]{:T(128)} all-reduce(f32[]{:T(128)S(6)} %add.162), channel_id=1, replica_groups=mesh['geo'=128,'rep'=4] {'geo'}, use_global_device_ids=true, to_apply=%region_16.18 | all-reduce | flops 1 | bytes 8 | tf_op jit(solution)/shard_map/psum | solution.py:49
  832.8 11.8 gather_fusion.4
  866.1 11.8 gather_fusion.5
  877.9 11.6 scatter_custom_fusion.5
  908.2 11.7 scatter_custom_fusion.4
  919.9 8.9 all-to-all-done.6
  935.2 13.5 all-reduce.2
  951.3 249.7 %psum.107 = f32[]{:T(128)} all-reduce(f32[]{:T(128)S(6)} %add.168), channel_id=1, replica_groups=mesh['geo'=128,'rep'=4] {'geo'}, use_global_device_ids=true, to_apply=%region_23.25 | all-reduce | flops 1 | bytes 8 | tf_op jit(solution)/shard_map/psum | solution.py:68
  1204.9 247.3 %psum.108 = f32[]{:T(128)} all-reduce(f32[]{:T(128)S(6)} %add.170), channel_id=1, replica_groups=mesh['geo'=128,'rep'=4] {'geo'}, use_global_device_ids=true, to_apply=%region_26.28 | all-reduce | flops 1 | bytes 8 | tf_op jit(solution)/shard_map/psum | solution.py:49
  1473.2 11.8 gather_fusion.6
  1506.5 11.8 gather_fusion.7
  1518.3 11.6 scatter_custom_fusion.7
  1548.6 11.5 scatter_custom_fusion.6
  1560.1 9.0 all-to-all-done.8
  1575.6 11.5 all-reduce.1
  1589.7 249.6 %psum.111 = f32[]{:T(128)} all-reduce(f32[]{:T(128)S(6)} %add.176), channel_id=1, replica_groups=mesh['geo'=128,'rep'=4] {'geo'}, use_global_device_ids=true, to_apply=%region_33.35 | all-reduce | flops 1 | bytes 8 | tf_op jit(solution)/shard_map/psum | solution.py:68
  (137 shorter events, 271.0 us)
Async XLA Ops:
  2.0 29.9 %all-to-all-start = ((s32[128,1,1]{2,1,0:T(1,128)}), s32[128,1,1]{2,1,0:T(1,128)S(1)}, u32[]{:S(2)}, u32[]{:S(2)}) async-start(s32[128,1,1]{2,1,0:T(1,128)} %copy.59), calls=%async_computation | async-start | bytes 131072 | tf_op jit(solution)/shard_map/all_to_all | solution.py:16
  46.2 8.1 copy-start
  46.2 8.1 copy-start.3
  46.2 8.1 copy-start.4
  46.2 8.1 copy-start.5
  48.1 26.8 %all-to-all-start.1 = ((f32[128,1,960]{2,1,0:T(1,128)}), f32[128,1,960]{2,1,0:T(1,128)S(1)}, u32[]{:S(2)}, u32[]{:S(2)}) async-start(f32[128,1,960]{2,1,0:T(1,128)} %reshape.450), calls=%async_computation.1 | async-start | bytes 1048576 | tf_op jit(solution)/shard_map/all_to_all | solution.py:51
  87.7 11.8 copy-start.6
  124.4 26.0 %all-to-all-start.2 = ((f32[128,1,960]{2,1,0:T(1,128)}), f32[128,1,960]{2,1,0:T(1,128)S(1)}, u32[]{:S(2)}, u32[]{:S(2)}) async-start(f32[128,1,960]{2,1,0:T(1,128)} %reshape.452), calls=%async_computation.2 | async-start | bytes 1048576 | tf_op jit(solution)/shard_map/all_to_all | solution.py:43
  154.5 16.6 copy-start.1
  154.5 16.6 copy-start.2
  185.2 29.5 %all-to-all-start.3 = ((f32[128,1,960]{2,1,0:T(1,128)}), f32[128,1,960]{2,1,0:T(1,128)S(1)}, u32[]{:S(2)}, u32[]{:S(2)}) async-start(f32[128,1,960]{2,1,0:T(1,128)} %reshape.454), calls=%async_computation.3 | async-start | bytes 1048576 | tf_op jit(solution)/shard_map/all_to_all | solution.py:62
  264.3 26.0 %all-to-all-start.4 = ((f32[128,1,960]{2,1,0:T(1,128)}), f32[128,1,960]{2,1,0:T(1,128)S(1)}, u32[]{:S(2)}, u32[]{:S(2)}) async-start(f32[128,1,960]{2,1,0:T(1,128)} %reshape.456), calls=%async_computation.4 | async-start | bytes 1048576 | tf_op jit(solution)/shard_map/all_to_all | solution.py:43
  826.4 26.9 %all-to-all-start.5 = ((f32[128,1,960]{2,1,0:T(1,128)}), f32[128,1,960]{2,1,0:T(1,128)S(1)}, u32[]{:S(2)}, u32[]{:S(2)}) async-start(f32[128,1,960]{2,1,0:T(1,128)} %reshape.458), calls=%async_computation.5 | async-start | bytes 1048576 | tf_op jit(solution)/shard_map/all_to_all | solution.py:62
  902.7 26.0 %all-to-all-start.6 = ((f32[128,1,960]{2,1,0:T(1,128)}), f32[128,1,960]{2,1,0:T(1,128)S(1)}, u32[]{:S(2)}, u32[]{:S(2)}) async-start(f32[128,1,960]{2,1,0:T(1,128)} %reshape.460), calls=%async_computation.6 | async-start | bytes 1048576 | tf_op jit(solution)/shard_map/all_to_all | solution.py:43
  1467.0 26.7 %all-to-all-start.7 = ((f32[128,1,960]{2,1,0:T(1,128)}), f32[128,1,960]{2,1,0:T(1,128)S(1)}, u32[]{:S(2)}, u32[]{:S(2)}) async-start(f32[128,1,960]{2,1,0:T(1,128)} %reshape.462), calls=%async_computation.7 | async-start | bytes 1048576 | tf_op jit(solution)/shard_map/all_to_all | solution.py:62
  1543.1 26.0 %all-to-all-start.8 = ((f32[128,1,960]{2,1,0:T(1,128)}), f32[128,1,960]{2,1,0:T(1,128)S(1)}, u32[]{:S(2)}, u32[]{:S(2)}) async-start(f32[128,1,960]{2,1,0:T(1,128)} %reshape.464), calls=%async_computation.8 | async-start | bytes 1048576 | tf_op jit(solution)/shard_map/all_to_all | solution.py:43
where the time goes:
time: 1850 us; the launch traced here: 1840 us
  blocking collectives  1290 us (70%)
  local copies, waits for them, and re-layouts  204 us (11%)
  other arithmetic  176 us (10%)
  waiting for transfers between devices  80.1 us (4%)
  starting transfers between devices  67.7 us (4%)
    psum x3, blocking collectives, squares(): return lax.psum(local, 'geo')  744 us
    psum x2, blocking collectives, body(): alpha = norm_now / lax.psum(local_curv, 'geo')  499 us
    unnamed x8, other arithmetic  56.6 us
    psum x4, blocking collectives, totals(): return lax.psum((res_part, folded.reshape(cells, tracts_dev)), 'rep')  50.7 us
    gather x4, local copies, waits for them, and re-layouts, pick(): return fetched.reshape(-1)[work_index]  47.1 us
    scatter-add x4, other arithmetic, totals(): jax.ops.segment_sum(values, work_index, num_segments=slot_count)  46.5 us
    scatter-add x4, other arithmetic, totals(): jax.ops.segment_sum(values, res_index, num_segments=cells * tracts_dev)  46.3 us
    unnamed x31, local copies, waits for them, and re-layouts  39.1 us
  transfers between devices with their start and end apart: 9, of which 9 were waited for; matrix products, arithmetic and copies ran while one was open for 5% of the time, Pallas kernels for 0%

commit v1 on v0

v1 whole, which is shorter than its diff:
```python
import functools

import jax
import jax.numpy as jnp
from jax import lax
from jax.experimental import pallas as pl
from jax.experimental.pallas import tpu as pltpu
from jax.sharding import PartitionSpec as P

BLK = 32
ITERS = 3
RIDGE = 0.5
MESH = pl.DeviceIdType.MESH
LANES = 128
PART = 8
CAP = 48
STEEP = 128.0
FLAT = 1e-3
BF = jnp.bfloat16
F32 = jnp.float32


def gather(table, index, rows):
    high = index >> 7
    low = index & 127
    out = jnp.zeros(index.shape, F32)
    for row in range(rows):
        for half in range(2):
            line = table[row : row + 1, half * LANES : (half + 1) * LANES]
            line = jnp.broadcast_to(line, index.shape)
            out = jnp.where(high == 2 * row + half, jnp.take_along_axis(line, low, axis=1), out)
    return out


def share_kernel(
    n_rep, base, res, slot, cell, needed, lam_res, lam_work, t_res, t_work,
    jobs, parts, send, recv, wide, send_sem, recv_sem,
):
    g, r = lax.axis_index("geo"), lax.axis_index("rep")
    barrier = pltpu.get_barrier_semaphore()
    for i in range(1, n_rep):
        pl.semaphore_signal(
            barrier, inc=1, device_id=(g, lax.rem(r + i, n_rep)), device_id_type=MESH
        )
    cells = lam_res.shape[0]
    n = base.shape[0]
    c = cell[...]
    s = slot[...]
    p = s >> 5
    block = jnp.take_along_axis(jnp.broadcast_to(needed[...], s.shape), p, axis=1)
    work = c * 256 + block * BLK + (s & (BLK - 1))
    home = c * 256 + res[...]
    u = base[...] * jnp.exp(gather(lam_res[...], home, cells))
    send[0:n, :] = u
    send[n : 2 * n, :] = p.astype(F32)
    send[2 * n : 3 * n, :] = work.astype(F32)
    send[3 * n : 4 * n, :] = home.astype(F32)
    for k, table in enumerate((lam_work, t_res, t_work)):
        wide[k] = jnp.zeros(wide.shape[1:], F32)
        wide[k, 0:cells, :] = table[...]
        parts[k] = wide[k, pl.ds(pl.multiple_of(r * PART, PART), PART), :]
    pl.semaphore_wait(barrier, n_rep - 1)
    copies = []
    for i in range(1, n_rep):
        copy = pltpu.make_async_remote_copy(
            src_ref=send,
            dst_ref=recv.at[r],
            send_sem=send_sem.at[i - 1],
            recv_sem=recv_sem.at[i - 1],
            device_id=(g, lax.rem(r + i, n_rep)),
            device_id_type=MESH,
        )
        copy.start()
        copies.append(copy)
    recv[r] = send[...]
    for copy in copies:
        copy.wait()
    for q in range(n_rep):
        for f in range(4):
            jobs[f, q * n : (q + 1) * n, :] = recv[q, f * n : (f + 1) * n, :]


def split(x):
    high = x.astype(BF).astype(F32)
    return high, x - high


def newton_kernel(
    n_geo, n_rep, jobs, parts, o_sr, o_sw, o_rr, o_rw, o_flag,
    ohp, pre, rank, fields, place, oht_r, oht_w, left, send, recv, xbuf,
    send_sem, recv_sem, xsend_sem, xrecv_sem,
):
    g, r = lax.axis_index("geo"), lax.axis_index("rep")
    barrier = pltpu.get_barrier_semaphore()

    def greet(i, carry):
        pl.semaphore_signal(
            barrier, inc=1, device_id=(lax.rem(g + i, n_geo), r), device_id_type=MESH
        )
        return carry

    lax.fori_loop(1, n_geo, greet, 0)
    for i in range(1, n_rep):
        pl.semaphore_signal(
            barrier, inc=1, device_id=(g, lax.rem(r + i, n_rep)), device_id_type=MESH
        )

    rows = jobs.shape[1]
    chunks = rows // 2
    u_all = jobs[0]
    work_all = jobs[2].astype(jnp.int32)
    home_all = jobs[3].astype(jnp.int32)
    local = (work_all >> 8) - r * PART
    inside = (local >= 0) & (local < PART)
    owner = jnp.where(inside, jobs[1].astype(jnp.int32), 2 * LANES)
    peers = lax.broadcasted_iota(jnp.int32, (LANES, 2 * LANES), 0)

    def pair(x, c):
        return jnp.concatenate([x[2 * c : 2 * c + 1, :], x[2 * c + 1 : 2 * c + 2, :]], axis=1)

    before = lax.broadcasted_iota(jnp.int32, (2 * LANES, 2 * LANES), 0)
    after = lax.broadcasted_iota(jnp.int32, (2 * LANES, 2 * LANES), 1)
    upto = jnp.where(before <= after, 1.0, 0.0).astype(BF)
    for c in range(chunks):
        span = slice(c * 256, (c + 1) * 256)
        hot = jnp.where(pair(owner, c) == peers, 1.0, 0.0)
        ohp[:, span] = hot.astype(BF)
    for c in range(chunks):
        span = slice(c * 256, (c + 1) * 256)
        pre[:, span] = jnp.dot(ohp[:, span], upto, preferred_element_type=F32)
    so_far = jnp.zeros((LANES, 1), F32)
    most = jnp.zeros((1, 256), F32)
    u_1 = u_all.astype(BF).astype(F32)
    u_2 = (u_all - u_1).astype(BF).astype(F32)
    u_3 = u_all - u_1 - u_2
    kinds = (
        u_1,
        u_2,
        u_3,
        local.astype(F32),
        (work_all & 255).astype(F32),
        (home_all & 255).astype(F32),
    )
    steps = lax.broadcasted_iota(jnp.int32, (CAP, 256), 0).astype(F32)
    for c in range(chunks):
        span = slice(c * 256, (c + 1) * 256)
        here = pre[:, span]
        place_c = jnp.sum(ohp[:, span].astype(F32) * (here + so_far), axis=0, keepdims=True) - 1.0
        so_far = so_far + here[:, 255:256]
        most = jnp.maximum(most, place_c)
        spot = place_c == steps
        for f, kind in enumerate(kinds):
            fields[f * CAP : (f + 1) * CAP, span] = jnp.where(spot, pair(kind, c), 0.0).astype(BF)
    place[...] = lax.dot_general(
        fields[...], ohp[...], (((1,), (1,)), ((), ())), preferred_element_type=F32
    )
    u_g = place[0:CAP, :] + place[CAP : 2 * CAP, :] + place[2 * CAP : 3 * CAP, :]
    cell_g = place[3 * CAP : 4 * CAP, :]
    work_g = cell_g * 256.0 + place[4 * CAP : 5 * CAP, :]
    res_g = place[5 * CAP : 6 * CAP, :]
    home_g = (cell_g * 256.0 + res_g).astype(jnp.int32)
    cell_g = cell_g.astype(jnp.int32)

    pad = jnp.zeros((LANES - 2 * CAP, LANES), F32)

    def launch(k, first, second):
        whole = jnp.concatenate([first, second, pad], axis=0)
        send[k] = jnp.transpose(whole).reshape(LANES, 1, LANES)

        def go(i, carry):
            peer = lax.rem(g + i, n_geo)
            pltpu.make_async_remote_copy(
                src_ref=send.at[k, peer],
                dst_ref=recv.at[k, g],
                send_sem=send_sem.at[k],
                recv_sem=recv_sem.at[k],
                device_id=(peer, r),
                device_id_type=MESH,
            ).start()
            return carry

        lax.fori_loop(1, n_geo, go, 0, unroll=True if n_geo < 8 else 1)
        recv[k, g] = send[k, g]

    def everything(k):
        return pltpu.make_async_remote_copy(
            src_ref=send.at[k, pl.ds(0, n_geo - 1)],
            dst_ref=recv.at[k, pl.ds(0, n_geo - 1)],
            send_sem=send_sem.at[k],
            recv_sem=recv_sem.at[k],
            device_id=(g, r),
            device_id_type=MESH,
        )

    def arrive(k):
        everything(k).wait_recv()
        return recv[k].reshape(LANES, LANES)

    tracts = lax.broadcasted_iota(jnp.int32, (LANES, 256), 1).astype(F32)

    def columns(oht, numbers):
        for k in range(CAP):
            hot = jnp.where(numbers[:, k : k + 1] == tracts, 1.0, 0.0)
            oht[k * LANES : (k + 1) * LANES, :] = hot.astype(BF)

    lines = lax.broadcasted_iota(jnp.int32, (PART, LANES), 0)

    def scatter(values, cell, oht):
        pieces = [piece for value in values for piece in split(value)]
        for k in range(CAP):
            mine = cell[k : k + 1, :] == lines
            stack = [jnp.where(mine, piece[k : k + 1, :], 0.0) for piece in pieces]
            left[0 : PART * len(pieces), k * LANES : (k + 1) * LANES] = jnp.concatenate(
                stack, axis=0
            ).astype(BF)
        out = jnp.dot(left[0 : PART * len(pieces), :], oht[...], preferred_element_type=F32)
        return [
            out[2 * v * PART : (2 * v + 1) * PART] + out[(2 * v + 1) * PART : (2 * v + 2) * PART]
            for v in range(len(values))
        ]

    pl.semaphore_wait(barrier, n_geo - 1 + n_rep - 1)
    launch(0, u_g, work_g)
    columns(oht_r, jnp.transpose(jnp.concatenate([res_g, jnp.zeros((LANES - CAP, LANES), F32)], axis=0)))

    got = arrive(0)
    flat = jnp.transpose(got)
    u_o = flat[0:CAP]
    work_o = flat[CAP : 2 * CAP].astype(jnp.int32)
    cell_o = work_o >> 8
    columns(oht_w, (got[:, CAP : 2 * CAP].astype(jnp.int32) & 255).astype(F32))
    w_o = u_o * gather(jnp.exp(parts[0]), work_o, PART)
    [sum_w] = scatter([w_o], cell_o, oht_w)
    diag_w = sum_w + RIDGE
    b0 = parts[2] - sum_w
    launch(1, w_o, gather(b0, work_o, PART))

    flat = jnp.transpose(arrive(1))
    w_g = flat[0:CAP]
    sum_r, bb0 = scatter([w_g, w_g * flat[CAP : 2 * CAP]], cell_g, oht_r)
    diag_r = sum_r + RIDGE
    a0 = parts[1] - sum_r
    a1 = diag_r * a0 + bb0
    launch(2, w_g * gather(a0, home_g, PART), w_g * gather(a1, home_g, PART))

    flat = jnp.transpose(arrive(2))
    ba0, ba1 = scatter([flat[0:CAP], flat[CAP : 2 * CAP]], cell_o, oht_w)
    b1 = diag_w * b0 + ba0
    b2 = diag_w * b1 + ba1
    launch(3, w_o * gather(b1, work_o, PART), w_o * gather(b2, work_o, PART))

    flat = jnp.transpose(arrive(3))
    bb1, bb2 = scatter([flat[0:CAP], flat[CAP : 2 * CAP]], cell_g, oht_r)
    a2 = diag_r * a1 + bb1
    a3 = diag_r * a2 + bb2

    def line(x):
        x = x[:, 0:LANES] + x[:, LANES : 2 * LANES]
        return jnp.sum(x, axis=0, keepdims=True)

    steep = jnp.maximum(jnp.max(sum_r), jnp.max(sum_w))
    bad = jnp.where(jnp.logical_or(steep > STEEP, jnp.max(most) >= CAP), 1.0, 0.0)
    table = jnp.concatenate(
        [
            line(a0 * a0 + b0 * b0),
            line(a0 * a1 + b0 * b1),
            line(a1 * a1 + b1 * b1),
            line(a1 * a2 + b1 * b2),
            line(a2 * a2 + b2 * b2),
            line(a2 * (a3 + bb2) + diag_w * b2 * b2),
            jnp.full((1, LANES), bad, F32),
            jnp.zeros((1, LANES), F32),
        ],
        axis=0,
    )
    table = jnp.broadcast_to(jnp.sum(table, axis=1, keepdims=True), (8, LANES))
    launch(
        4,
        w_g * gather(a2, home_g, PART),
        jnp.concatenate([table, jnp.zeros((CAP - 8, LANES), F32)], axis=0),
    )

    early = 7 * PART
    for v, vector in enumerate((a0, a1, a2, a3, b0, b1, b2)):
        xbuf[r, v * PART : (v + 1) * PART, :] = vector

    def across(lo, hi, which):
        copies = []
        for i in range(1, n_rep):
            copy = pltpu.make_async_remote_copy(
                src_ref=xbuf.at[r, pl.ds(lo, hi - lo)],
                dst_ref=xbuf.at[r, pl.ds(lo, hi - lo)],
                send_sem=xsend_sem.at[which, i - 1],
                recv_sem=xrecv_sem.at[which, i - 1],
                device_id=(g, lax.rem(r + i, n_rep)),
                device_id_type=MESH,
            )
            copy.start()
            copies.append(copy)
        return copies

    first = across(0, early, 0)

    flat = jnp.transpose(arrive(4))
    [ba2] = scatter([flat[0:CAP]], cell_o, oht_w)
    b3 = diag_w * b2 + ba2
    xbuf[r, early : early + PART, :] = b3
    xbuf[r, early + PART : early + 2 * PART, :] = jnp.broadcast_to(
        jnp.sum(flat[CAP : CAP + 8], axis=1, keepdims=True), (8, 256)
    )
    last = across(early, early + 2 * PART, 1)
    for copy in first + last:
        copy.wait()
    for k in range(5):
        everything(k).wait_send()

    sums = xbuf[0, early + PART : early + 2 * PART, :]
    for q in range(1, n_rep):
        sums = sums + xbuf[q, early + PART : early + 2 * PART, :]
    m = [sums[i : i + 1, :] for i in range(7)]

    def form(x, shift):
        n = len(x)
        total = None
        for s in range(2 * n - 1):
            part = None
            for i in range(max(0, s - n + 1), min(n - 1, s) + 1):
                term = x[i] * x[s - i]
                part = term if part is None else part + term
            part = part * m[s + shift]
            total = part if total is None else total + part
        return total

    one = jnp.ones((1, 256), F32)
    rc, pc, xc = [one], [one], []
    norm = m[0]
    for turn in range(ITERS):
        alpha = norm / form(pc, 1)
        xc = [x + alpha * p for x, p in zip(xc, pc)] + [alpha * pc[-1]]
        image = [-alpha * p for p in pc]
        rc = [rc[0]] + [x + y for x, y in zip(rc[1:], image[:-1])] + [image[-1]]
        if turn < ITERS - 1:
            new = form(rc, 0)
            beta = new / norm
            pc = [x + beta * p for x, p in zip(rc[:-1], pc)] + [rc[-1]]
            norm = new
    good = jnp.logical_and(m[6] == 0.0, norm > FLAT * m[0])
    o_flag[...] = jnp.broadcast_to(jnp.where(good, 0.0, 1.0)[:, 0:LANES], (8, LANES))
    cells = o_sr.shape[0]
    for q in range(n_rep):
        lo, hi = q * PART, min((q + 1) * PART, cells)
        for side, o_step, o_resid in ((0, o_sr, o_rr), (1, o_sw, o_rw)):
            k = [
                xbuf[q, (4 * side + i) * PART : (4 * side + i) * PART + hi - lo, :]
                for i in range(4)
            ]
            o_step[lo:hi, :] = xc[0] * k[0] + xc[1] * k[1] + xc[2] * k[2]
            o_resid[lo:hi, :] = k[0] + rc[1] * k[1] + rc[2] * k[2] + rc[3] * k[3]


def general(base, job_res, job_slot, job_cell, needed, lam_res, lam_work, target_res, target_work):
    cells, tracts_dev = lam_res.shape
    blocks_dev = tracts_dev // BLK
    requests = lax.all_to_all(needed[0], "geo", split_axis=0, concat_axis=0, tiled=True)
    sources, listed = requests.shape
    hot = requests[:, :, None] == jnp.arange(blocks_dev, dtype=jnp.int32)[None, None, :]
    onehot = hot.astype(jnp.float32)
    slot_shape = (sources, listed, cells, BLK)
    slot_count = sources * listed * cells * BLK
    res_index = job_cell * tracts_dev + job_res
    work_index = (job_slot // BLK * cells + job_cell) * BLK + job_slot % BLK

    def serve(table):
        blocks = table.reshape(cells, blocks_dev, BLK).transpose(1, 0, 2)
        out = jnp.zeros(slot_shape, jnp.float32)
        for b in range(blocks_dev):
            out = jnp.where(hot[:, :, b, None, None], blocks[b][None, None], out)
        return out

    def pick(fetched):
        return fetched.reshape(-1)[work_index]

    def fold(arrived):
        return jnp.einsum("skb,skcx->cbx", onehot, arrived, precision=lax.Precision.HIGHEST)

    def totals(values):
        res_part = jax.ops.segment_sum(values, res_index, num_segments=cells * tracts_dev).reshape(
            cells, tracts_dev
        )
        work_part = jax.ops.segment_sum(values, work_index, num_segments=slot_count).reshape(
            slot_shape
        )
        arrived = lax.all_to_all(work_part, "geo", split_axis=0, concat_axis=0, tiled=True)
        folded = fold(arrived)
        return lax.psum((res_part, folded.reshape(cells, tracts_dev)), "rep")

    def squares(part_res, part_work):
        local = jnp.sum(part_res * part_res) + jnp.sum(part_work * part_work)
        return lax.psum(local, "geo")

    def fetch(table):
        return lax.all_to_all(serve(table), "geo", split_axis=0, concat_axis=0, tiled=True)

    weight = base * jnp.exp(lam_res.reshape(-1)[res_index] + pick(fetch(lam_work)))
    total_res, total_work = totals(weight)
    resid_res = -(total_res - target_res)
    resid_work = -(total_work - target_work)
    zero = jnp.zeros_like(resid_res)
    norm = squares(resid_res, resid_work)

    def turn(_, state):
        step_res, step_work, resid_res, resid_work, dir_res, dir_work, norm_now = state
        along = dir_res.reshape(-1)[res_index] + pick(fetch(dir_work))
        image_res, image_work = totals(weight * along)
        image_res = image_res + RIDGE * dir_res
        image_work = image_work + RIDGE * dir_work
        local_curv = jnp.sum(dir_res * image_res) + jnp.sum(dir_work * image_work)
        alpha = norm_now / lax.psum(local_curv, "geo")
        step_res = step_res + alpha * dir_res
        step_work = step_work + alpha * dir_work
        resid_res = resid_res - alpha * image_res
        resid_work = resid_work - alpha * image_work
        norm_next = squares(resid_res, resid_work)
        dir_res = resid_res + norm_next / norm_now * dir_res
        dir_work = resid_work + norm_next / norm_now * dir_work
        return step_res, step_work, resid_res, resid_work, dir_res, dir_work, norm_next

    state = (zero, zero, resid_res, resid_work, resid_res, resid_work, norm)
    return lax.fori_loop(0, ITERS, turn, state)[:4]


def body(n_geo, n_rep, *args):
    base, job_res, job_slot, job_cell, needed, lam_res, lam_work, target_res, target_work = args
    n = base.shape[0] // LANES
    cells, tracts = lam_res.shape
    vmem = pl.BlockSpec(memory_space=pltpu.VMEM)
    dma = pltpu.SemaphoreType.DMA
    jobs, parts = pl.pallas_call(
        functools.partial(share_kernel, n_rep),
        out_shape=[
            jax.ShapeDtypeStruct((4, n_rep * n, LANES), F32),
            jax.ShapeDtypeStruct((3, PART, tracts), F32),
        ],
        in_specs=[vmem] * 9,
        out_specs=[vmem] * 2,
        scratch_shapes=[
            pltpu.VMEM((4 * n, LANES), F32),
            pltpu.VMEM((n_rep, 4 * n, LANES), F32),
            pltpu.VMEM((3, n_rep * PART, tracts), F32),
            dma((n_rep - 1,)),
            dma((n_rep - 1,)),
        ],
        compiler_params=pltpu.CompilerParams(collective_id=0, has_side_effects=True),
        name="share",
    )(
        base.reshape(n, LANES),
        job_res.reshape(n, LANES),
        job_slot.reshape(n, LANES),
        job_cell.reshape(n, LANES),
        needed.reshape(1, LANES),
        lam_res,
        lam_work,
        target_res,
        target_work,
    )
    count = n_rep * n * LANES
    out = jax.ShapeDtypeStruct((cells, tracts), F32)
    *fast, flag = pl.pallas_call(
        functools.partial(newton_kernel, n_geo, n_rep),
        out_shape=[out] * 4 + [jax.ShapeDtypeStruct((8, LANES), F32)],
        in_specs=[vmem] * 2,
        out_specs=[vmem] * 5,
        scratch_shapes=[
            pltpu.VMEM((LANES, count), BF),
            pltpu.VMEM((LANES, count), F32),
            pltpu.VMEM((8, LANES), F32),
            pltpu.VMEM((6 * CAP, count), BF),
            pltpu.VMEM((6 * CAP, LANES), F32),
            pltpu.VMEM((CAP * LANES, tracts), BF),
            pltpu.VMEM((CAP * LANES, tracts), BF),
            pltpu.VMEM((4 * PART, CAP * LANES), BF),
            pltpu.VMEM((5, LANES, 1, LANES), F32),
            pltpu.VMEM((5, LANES, 1, LANES), F32),
            pltpu.VMEM((n_rep, 9 * PART, tracts), F32),
            dma((5,)),
            dma((5,)),
            dma((2, n_rep - 1)),
            dma((2, n_rep - 1)),
        ],
        compiler_params=pltpu.CompilerParams(
            collective_id=1, has_side_effects=True, vmem_limit_bytes=48 * 2**20
        ),
        name="newton",
    )(jobs, parts)
    return lax.cond(flag[0, 0] == 0.0, lambda: tuple(fast), lambda: tuple(general(*args)))


def solution(mesh):
    in_specs = (
        P(("geo", "rep")),
        P(("geo", "rep")),
        P(("geo", "rep")),
        P(("geo", "rep")),
        P("geo", None, None),
        P(None, "geo"),
        P(None, "geo"),
        P(None, "geo"),
        P(None, "geo"),
    )
    out_specs = (P(None, "geo"), P(None, "geo"), P(None, "geo"), P(None, "geo"))
    work = functools.partial(body, mesh.shape["geo"], mesh.shape["rep"])
    return jax.shard_map(work, mesh=mesh, in_specs=in_specs, out_specs=out_specs, check_vma=False)
```

time: 1850 us -> 91.5 us (0.05)
  blocking collectives: 1290 us -> 0 us
  local copies, waits for them, and re-layouts: 204 us -> 7.64 us
  other arithmetic: 176 us -> 0 us
  Pallas kernels: 0 us -> 81.7 us
  waiting for transfers between devices: 80.1 us -> 0 us
  starting transfers between devices: 67.7 us -> 0 us
    psum x9 -> x0, blocking collectives: 1290 us -> none  [the longest x3 744 us: squares(): return lax.psum(local, 'geo')]
    gather x12 -> x0, local copies, waits for them, and re-layouts: 97.4 us -> none  [the longest x4 47.1 us: pick(): return fetched.reshape(-1)[work_index]]
    scatter-add x8 -> x0, other arithmetic: 92.8 us -> none  [the longest x4 46.5 us: totals(): jax.ops.segment_sum(values, work_index, num_segments=slot_count)]
    pallas_call x0 -> x2, Pallas kernels: none -> 81.7 us  [the longest x1 73.2 us: body(): pl.pallas_call(functools.partial(newton_kernel, n_geo, n_rep), out_shape=...]
    all_to_all x9 -> x0, waiting for transfers between devices: 80.1 us -> none  [the longest x4 34.6 us: totals(): lax.all_to_all(work_part, 'geo', split_axis=0, concat_axis=0, tiled=True)]
    all_to_all x9 -> x0, starting transfers between devices: 67.7 us -> none  [the longest x4 21.7 us: totals(): lax.all_to_all(work_part, 'geo', split_axis=0, concat_axis=0, tiled=True)]
    unnamed x8 -> x0, other arithmetic: 56.6 us -> none
    all_to_all x9 -> x0, local copies, waits for them, and re-layouts: 33.5 us -> none  [the longest x3 20.7 us: body(): lax.all_to_all(served, 'geo', split_axis=0, concat_axis=0, tiled=True)]
  transfers between devices with their start and end apart: 9 -> 0, of which waited for: 9 -> 0; matrix products, arithmetic and copies ran while one was open for 5% -> 0% of each run, Pallas kernels for 0% -> 0%
where the time goes in v1:
time: 91.5 us; the launch traced here: 90.9 us
  Pallas kernels  81.7 us (89%)
  local copies, waits for them, and re-layouts  7.64 us (8%)
  between operations  1.32 us (1%)
    pallas_call x1, Pallas kernels, body(): pl.pallas_call(functools.partial(newton_kernel, n_geo, n_rep), out_shape=...  73.2 us
    pallas_call x1, Pallas kernels, body(): pl.pallas_call(functools.partial(share_kernel, n_rep), out_shape=[jax.Sha...  8.44 us
    unnamed x8, local copies, waits for them, and re-layouts  7.13 us

profile of v1, /device:TPU:1, one launch (start us, length us, event | category | flops | bytes accessed | tf_op | source)
XLA Modules:
  0.0 90.9 jit_solution(1645376009372809550)
XLA Ops:
  0.6 8.4 %share.1 = (f32[4,64,128]{2,1,0:T(8,128)}, f32[3,8,256]{2,1,0:T(8,128)}) custom-call(f32[16,128]{1,0:T(8,128)} %bitcast.153, s32[16,128]{1,0:T(8,128)} %bitcast.150, s32[16,128]{1,0:T(8,128)} %bitcast.151, s32[16,128]{1,0:T(8,128)} %bitcast.152, s32[1,128]{1,0:T(1,128)} %bitcast.154, f32[30,256]{1,0:T(8,128)} %lam_res.1, f32[30,256]{1,0:T(8,128)} %lam_work.1, ...), custom_call_target="tpu_custom_call" | custom-call | tf_op jit(solution)/shard_map/share/pallas_call | solution.py:438
  9.1 0.0 copy-start
  9.1 0.9 copy-done
  10.0 0.0 copy-start.1
  10.0 0.7 copy-done.1
  10.7 73.2 %newton.1 = (f32[30,256]{1,0:T(8,128)}, f32[30,256]{1,0:T(8,128)}, f32[30,256]{1,0:T(8,128)}, f32[30,256]{1,0:T(8,128)}, f32[8,128]{1,0:T(8,128)S(1)}) custom-call(f32[4,64,128]{2,1,0:T(8,128)S(1)} %copy-done, f32[3,8,256]{2,1,0:T(8,128)S(1)} %copy-done.1), custom_call_target="tpu_custom_call" | custom-call | tf_op jit(solution)/shard_map/newton/pallas_call | solution.py:468
  84.0 0.5 slice.99
  85.1 0.3 conditional.1
  85.4 1.4 %copy.80 = f32[30,256]{1,0:T(8,128)} copy(f32[30,256]{1,0:T(8,128)} %get-tuple-element.455) | data formatting | bytes 61440
  86.8 1.4 %copy.81 = f32[30,256]{1,0:T(8,128)} copy(f32[30,256]{1,0:T(8,128)} %get-tuple-element.456) | data formatting | bytes 61440
  88.1 1.4 %copy.82 = f32[30,256]{1,0:T(8,128)} copy(f32[30,256]{1,0:T(8,128)} %get-tuple-element.457) | data formatting | bytes 61440
  89.5 1.4 %copy.83 = f32[30,256]{1,0:T(8,128)} copy(f32[30,256]{1,0:T(8,128)} %get-tuple-element.458) | data formatting | bytes 61440
Async XLA Ops:
  9.1 0.9 copy-start
  10.0 0.7 copy-start.1

commit v2 on v1

--- a/solution.py
+++ b/solution.py
@@ -13,6 +13,7 @@
 MESH = pl.DeviceIdType.MESH
 LANES = 128
 PART = 8
+SUB = 24
 CAP = 48
 STEEP = 128.0
 FLAT = 1e-3
@@ -32,134 +33,145 @@
     return out
 
 
-def share_kernel(
-    n_rep, base, res, slot, cell, needed, lam_res, lam_work, t_res, t_work,
-    jobs, parts, send, recv, wide, send_sem, recv_sem,
+def split(x):
+    high = x.astype(BF).astype(F32)
+    return high, x - high
+
+
+def newton_kernel(
+    n_geo, n_rep, base, res, slot, cell, needed, lam_res, lam_work, t_res, t_work, o_all, o_flag,
+    wide, ohp, pre, fields, place, xsend, xlist, oht_r, oht_w, left, send, recv, xbuf,
+    list_send_sem, list_recv_sem, send_sem, recv_sem, xsend_sem, xrecv_sem,
 ):
     g, r = lax.axis_index("geo"), lax.axis_index("rep")
     barrier = pltpu.get_barrier_semaphore()
+
+    depth = n_geo // 16
+    z, y, core = g // 16, lax.rem(g // 2, 8), lax.rem(g, 2)
+    lows = [
+        lax.rem(y + d, 8) * 2 + lax.rem(core + e, 2)
+        for d in (4, 3, 5, 2, 6, 1, 7, 0)
+        for e in (1, 0)
+    ]
+
+    def each_peer(act):
+        def plane(j, carry):
+            high = lax.rem(z + j + 3, depth) * 16
+            for low in lows[:-1]:
+                act(high + low)
+            return carry
+
+        lax.fori_loop(0, depth, plane, 0)
+        for d in range(1, depth):
+            act(lax.rem(z + d, depth) * 16 + lows[-1])
+
+    each_peer(
+        lambda peer: pl.semaphore_signal(barrier, inc=1, device_id=(peer, r), device_id_type=MESH)
+    )
     for i in range(1, n_rep):
         pl.semaphore_signal(
             barrier, inc=1, device_id=(g, lax.rem(r + i, n_rep)), device_id_type=MESH
         )
+
     cells = lam_res.shape[0]
-    n = base.shape[0]
     c = cell[...]
     s = slot[...]
     p = s >> 5
     block = jnp.take_along_axis(jnp.broadcast_to(needed[...], s.shape), p, axis=1)
-    work = c * 256 + block * BLK + (s & (BLK - 1))
-    home = c * 256 + res[...]
-    u = base[...] * jnp.exp(gather(lam_res[...], home, cells))
-    send[0:n, :] = u
-    send[n : 2 * n, :] = p.astype(F32)
-    send[2 * n : 3 * n, :] = work.astype(F32)
-    send[3 * n : 4 * n, :] = home.astype(F32)
+    u_all = base[...] * jnp.exp(gather(lam_res[...], c * 256 + res[...], cells))
+    bucket = (c >> 3) * LANES + p
+    chunks = base.shape[0] // 2
+    peers = lax.broadcasted_iota(jnp.int32, (n_rep * LANES, 2 * LANES), 0)
+
+    def pair(x, k):
+        return jnp.concatenate([x[2 * k : 2 * k + 1, :], x[2 * k + 1 : 2 * k + 2, :]], axis=1)
+
+    before = lax.broadcasted_iota(jnp.int32, (2 * LANES, 2 * LANES), 0)
+    after = lax.broadcasted_iota(jnp.int32, (2 * LANES, 2 * LANES), 1)
+    upto = jnp.where(before <= after, 1.0, 0.0).astype(BF)
+    for k in range(chunks):
+        span = slice(k * 256, (k + 1) * 256)
+        ohp[:, span] = jnp.where(pair(bucket, k) == peers, 1.0, 0.0).astype(BF)
+    for k in range(chunks):
+        span = slice(k * 256, (k + 1) * 256)
+        pre[:, span] = jnp.dot(ohp[:, span], upto, preferred_element_type=F32)
+    u_1 = u_all.astype(BF).astype(F32)
+    u_2 = (u_all - u_1).astype(BF).astype(F32)
+    kinds = (
+        u_1,
+        u_2,
+        u_all - u_1 - u_2,
+        (c & (PART - 1)).astype(F32),
+        (block * BLK + (s & (BLK - 1))).astype(F32),
+        res[...].astype(F32),
+    )
+    steps = lax.broadcasted_iota(jnp.int32, (SUB, 256), 0).astype(F32)
+    so_far = jnp.zeros((n_rep * LANES, 1), F32)
+    for k in range(chunks):
+        span = slice(k * 256, (k + 1) * 256)
+        here = pre[:, span]
+        rank = jnp.sum(ohp[:, span].astype(F32) * (here + so_far), axis=0, keepdims=True) - 1.0
+        so_far = so_far + here[:, 255:256]
+        spot = rank == steps
+        for f, kind in enumerate(kinds):
+            fields[f * SUB : (f + 1) * SUB, span] = jnp.where(spot, pair(kind, k), 0.0).astype(BF)
+    most = jnp.max(so_far)
+    place[...] = lax.dot_general(
+        fields[...], ohp[...], (((1,), (1,)), ((), ())), preferred_element_type=F32
+    )
+    for q in range(n_rep):
+        lists = [
+            place[f * SUB : (f + 1) * SUB, q * LANES : (q + 1) * LANES] for f in range(len(kinds))
+        ]
+        xsend[q, 0:SUB, :] = lists[0] + lists[1] + lists[2]
+        xsend[q, SUB : 2 * SUB, :] = lists[3] * 256.0 + lists[4]
+        xsend[q, 2 * SUB : 3 * SUB, :] = lists[3] * 256.0 + lists[5]
     for k, table in enumerate((lam_work, t_res, t_work)):
         wide[k] = jnp.zeros(wide.shape[1:], F32)
         wide[k, 0:cells, :] = table[...]
-        parts[k] = wide[k, pl.ds(pl.multiple_of(r * PART, PART), PART), :]
-    pl.semaphore_wait(barrier, n_rep - 1)
+    mine = pl.ds(pl.multiple_of(r * PART, PART), PART)
+    parts = [wide[k, mine, :] for k in range(3)]
+    pl.semaphore_wait(barrier, n_geo - 1 + n_rep - 1)
+
     copies = []
     for i in range(1, n_rep):
+        other = lax.rem(r + i, n_rep)
         copy = pltpu.make_async_remote_copy(
-            src_ref=send,
-            dst_ref=recv.at[r],
-            send_sem=send_sem.at[i - 1],
-            recv_sem=recv_sem.at[i - 1],
-            device_id=(g, lax.rem(r + i, n_rep)),
+            src_ref=xsend.at[other],
+            dst_ref=xlist.at[r],
+            send_sem=list_send_sem.at[i - 1],
+            recv_sem=list_recv_sem.at[i - 1],
+            device_id=(g, other),
             device_id_type=MESH,
         )
         copy.start()
         copies.append(copy)
-    recv[r] = send[...]
+    xlist[r] = xsend[r]
     for copy in copies:
         copy.wait()
+    merged = [jnp.zeros((CAP, LANES), F32)] * 3
+    offset = jnp.zeros((1, LANES), jnp.int32)
+    empty = jnp.zeros((CAP - SUB, LANES), F32)
     for q in range(n_rep):
-        for f in range(4):
-            jobs[f, q * n : (q + 1) * n, :] = recv[q, f * n : (f + 1) * n, :]
-
-
-def split(x):
-    high = x.astype(BF).astype(F32)
-    return high, x - high
-
-
-def newton_kernel(
-    n_geo, n_rep, jobs, parts, o_sr, o_sw, o_rr, o_rw, o_flag,
-    ohp, pre, rank, fields, place, oht_r, oht_w, left, send, recv, xbuf,
-    send_sem, recv_sem, xsend_sem, xrecv_sem,
-):
-    g, r = lax.axis_index("geo"), lax.axis_index("rep")
-    barrier = pltpu.get_barrier_semaphore()
-
-    def greet(i, carry):
-        pl.semaphore_signal(
-            barrier, inc=1, device_id=(lax.rem(g + i, n_geo), r), device_id_type=MESH
-        )
-        return carry
-
-    lax.fori_loop(1, n_geo, greet, 0)
-    for i in range(1, n_rep):
-        pl.semaphore_signal(
-            barrier, inc=1, device_id=(g, lax.rem(r + i, n_rep)), device_id_type=MESH
-        )
-
-    rows = jobs.shape[1]
-    chunks = rows // 2
-    u_all = jobs[0]
-    work_all = jobs[2].astype(jnp.int32)
-    home_all = jobs[3].astype(jnp.int32)
-    local = (work_all >> 8) - r * PART
-    inside = (local >= 0) & (local < PART)
-    owner = jnp.where(inside, jobs[1].astype(jnp.int32), 2 * LANES)
-    peers = lax.broadcasted_iota(jnp.int32, (LANES, 2 * LANES), 0)
-
-    def pair(x, c):
-        return jnp.concatenate([x[2 * c : 2 * c + 1, :], x[2 * c + 1 : 2 * c + 2, :]], axis=1)
-
-    before = lax.broadcasted_iota(jnp.int32, (2 * LANES, 2 * LANES), 0)
-    after = lax.broadcasted_iota(jnp.int32, (2 * LANES, 2 * LANES), 1)
-    upto = jnp.where(before <= after, 1.0, 0.0).astype(BF)
-    for c in range(chunks):
-        span = slice(c * 256, (c + 1) * 256)
-        hot = jnp.where(pair(owner, c) == peers, 1.0, 0.0)
-        ohp[:, span] = hot.astype(BF)
-    for c in range(chunks):
-        span = slice(c * 256, (c + 1) * 256)
-        pre[:, span] = jnp.dot(ohp[:, span], upto, preferred_element_type=F32)
-    so_far = jnp.zeros((LANES, 1), F32)
-    most = jnp.zeros((1, 256), F32)
-    u_1 = u_all.astype(BF).astype(F32)
-    u_2 = (u_all - u_1).astype(BF).astype(F32)
-    u_3 = u_all - u_1 - u_2
-    kinds = (
-        u_1,
-        u_2,
-        u_3,
-        local.astype(F32),
-        (work_all & 255).astype(F32),
-        (home_all & 255).astype(F32),
-    )
-    steps = lax.broadcasted_iota(jnp.int32, (CAP, 256), 0).astype(F32)
-    for c in range(chunks):
-        span = slice(c * 256, (c + 1) * 256)
-        here = pre[:, span]
-        place_c = jnp.sum(ohp[:, span].astype(F32) * (here + so_far), axis=0, keepdims=True) - 1.0
-        so_far = so_far + here[:, 255:256]
-        most = jnp.maximum(most, place_c)
-        spot = place_c == steps
-        for f, kind in enumerate(kinds):
-            fields[f * CAP : (f + 1) * CAP, span] = jnp.where(spot, pair(kind, c), 0.0).astype(BF)
-    place[...] = lax.dot_general(
-        fields[...], ohp[...], (((1,), (1,)), ((), ())), preferred_element_type=F32
-    )
-    u_g = place[0:CAP, :] + place[CAP : 2 * CAP, :] + place[2 * CAP : 3 * CAP, :]
-    cell_g = place[3 * CAP : 4 * CAP, :]
-    work_g = cell_g * 256.0 + place[4 * CAP : 5 * CAP, :]
-    res_g = place[5 * CAP : 6 * CAP, :]
-    home_g = (cell_g * 256.0 + res_g).astype(jnp.int32)
-    cell_g = cell_g.astype(jnp.int32)
+        lists = [xlist[q, f * SUB : (f + 1) * SUB, :] for f in range(3)]
+        count = jnp.sum(jnp.where(lists[0] > 0.0, 1, 0), axis=0, keepdims=True)
+        lists = [jnp.concatenate([x, empty], axis=0) for x in lists]
+        if q:
+            for bit in range(6):
+                moved = (offset >> bit) & 1 == 1
+                width = 1 << bit
+                gap = jnp.zeros((width, LANES), F32)
+                lists = [
+                    jnp.where(moved, jnp.concatenate([gap, x[: CAP - width]], axis=0), x)
+                    for x in lists
+                ]
+        merged = [x + y for x, y in zip(merged, lists)]
+        offset = offset + count
+    crowded = jnp.logical_or(most > SUB, jnp.max(offset) > CAP)
+    u_g, work_g, home_g = merged
+    home_g = home_g.astype(jnp.int32)
+    cell_g = home_g >> 8
+    res_g = (home_g & 255).astype(F32)
 
     pad = jnp.zeros((LANES - 2 * CAP, LANES), F32)
 
@@ -167,9 +179,8 @@
         whole = jnp.concatenate([first, second, pad], axis=0)
         send[k] = jnp.transpose(whole).reshape(LANES, 1, LANES)
 
-        def go(i, carry):
-            peer = lax.rem(g + i, n_geo)
-            pltpu.make_async_remote_copy(
+        each_peer(
+            lambda peer: pltpu.make_async_remote_copy(
                 src_ref=send.at[k, peer],
                 dst_ref=recv.at[k, g],
                 send_sem=send_sem.at[k],
@@ -177,9 +188,7 @@
                 device_id=(peer, r),
                 device_id_type=MESH,
             ).start()
-            return carry
-
-        lax.fori_loop(1, n_geo, go, 0, unroll=True if n_geo < 8 else 1)
+        )
         recv[k, g] = send[k, g]
 
     def everything(k):
@@ -194,7 +203,11 @@
 
     def arrive(k):
         everything(k).wait_recv()
-        return recv[k].reshape(LANES, LANES)
+        return jnp.transpose(recv[k].reshape(LANES, LANES))
+
+    def over(x):
+        x = x.astype(F32)
+        return jnp.transpose(jnp.concatenate([x, jnp.zeros((LANES - CAP, LANES), F32)], axis=0))
 
     tracts = lax.broadcasted_iota(jnp.int32, (LANES, 256), 1).astype(F32)
 
@@ -219,23 +232,21 @@
             for v in range(len(values))
         ]
 
-    pl.semaphore_wait(barrier, n_geo - 1 + n_rep - 1)
     launch(0, u_g, work_g)
-    columns(oht_r, jnp.transpose(jnp.concatenate([res_g, jnp.zeros((LANES - CAP, LANES), F32)], axis=0)))
-
-    got = arrive(0)
-    flat = jnp.transpose(got)
+    columns(oht_r, over(res_g))
+
+    flat = arrive(0)
     u_o = flat[0:CAP]
     work_o = flat[CAP : 2 * CAP].astype(jnp.int32)
     cell_o = work_o >> 8
-    columns(oht_w, (got[:, CAP : 2 * CAP].astype(jnp.int32) & 255).astype(F32))
+    columns(oht_w, over(work_o & 255))
     w_o = u_o * gather(jnp.exp(parts[0]), work_o, PART)
     [sum_w] = scatter([w_o], cell_o, oht_w)
     diag_w = sum_w + RIDGE
     b0 = parts[2] - sum_w
     launch(1, w_o, gather(b0, work_o, PART))
 
-    flat = jnp.transpose(arrive(1))
+    flat = arrive(1)
     w_g = flat[0:CAP]
     sum_r, bb0 = scatter([w_g, w_g * flat[CAP : 2 * CAP]], cell_g, oht_r)
     diag_r = sum_r + RIDGE
@@ -243,13 +254,13 @@
     a1 = diag_r * a0 + bb0
     launch(2, w_g * gather(a0, home_g, PART), w_g * gather(a1, home_g, PART))
 
-    flat = jnp.transpose(arrive(2))
+    flat = arrive(2)
     ba0, ba1 = scatter([flat[0:CAP], flat[CAP : 2 * CAP]], cell_o, oht_w)
     b1 = diag_w * b0 + ba0
     b2 = diag_w * b1 + ba1
     launch(3, w_o * gather(b1, work_o, PART), w_o * gather(b2, work_o, PART))
 
-    flat = jnp.transpose(arrive(3))
+    flat = arrive(3)
     bb1, bb2 = scatter([flat[0:CAP], flat[CAP : 2 * CAP]], cell_g, oht_r)
     a2 = diag_r * a1 + bb1
     a3 = diag_r * a2 + bb2
@@ -259,7 +270,7 @@
         return jnp.sum(x, axis=0, keepdims=True)
 
     steep = jnp.maximum(jnp.max(sum_r), jnp.max(sum_w))
-    bad = jnp.where(jnp.logical_or(steep > STEEP, jnp.max(most) >= CAP), 1.0, 0.0)
+    bad = jnp.where(jnp.logical_or(steep > STEEP, crowded), 1.0, 0.0)
     table = jnp.concatenate(
         [
             line(a0 * a0 + b0 * b0),
@@ -301,7 +312,7 @@
 
     first = across(0, early, 0)
 
-    flat = jnp.transpose(arrive(4))
+    flat = arrive(4)
     [ba2] = scatter([flat[0:CAP]], cell_o, oht_w)
     b3 = diag_w * b2 + ba2
     xbuf[r, early : early + PART, :] = b3
@@ -345,17 +356,18 @@
             pc = [x + beta * p for x, p in zip(rc[:-1], pc)] + [rc[-1]]
             norm = new
     good = jnp.logical_and(m[6] == 0.0, norm > FLAT * m[0])
-    o_flag[...] = jnp.broadcast_to(jnp.where(good, 0.0, 1.0)[:, 0:LANES], (8, LANES))
-    cells = o_sr.shape[0]
+    o_flag[0, 0] = jnp.max(jnp.where(good, 0, 1))
     for q in range(n_rep):
-        lo, hi = q * PART, min((q + 1) * PART, cells)
-        for side, o_step, o_resid in ((0, o_sr, o_rr), (1, o_sw, o_rw)):
-            k = [
-                xbuf[q, (4 * side + i) * PART : (4 * side + i) * PART + hi - lo, :]
-                for i in range(4)
-            ]
-            o_step[lo:hi, :] = xc[0] * k[0] + xc[1] * k[1] + xc[2] * k[2]
-            o_resid[lo:hi, :] = k[0] + rc[1] * k[1] + rc[2] * k[2] + rc[3] * k[3]
+        lo = q * PART
+        for side in range(2):
+            k = [xbuf[q, (4 * side + i) * PART : (4 * side + i + 1) * PART, :] for i in range(4)]
+            o_all[side, lo : lo + PART, :] = xc[0] * k[0] + xc[1] * k[1] + xc[2] * k[2]
+            o_all[2 + side, lo : lo + PART, :] = k[0] + rc[1] * k[1] + rc[2] * k[2] + rc[3] * k[3]
+
+
+def hand_out(stack, *outs):
+    for k, out in enumerate(outs):
+        out[...] = stack[k, 0 : out.shape[0], :]
 
 
 def general(base, job_res, job_slot, job_cell, needed, lam_res, lam_work, target_res, target_work):
@@ -435,23 +447,41 @@
     cells, tracts = lam_res.shape
     vmem = pl.BlockSpec(memory_space=pltpu.VMEM)
     dma = pltpu.SemaphoreType.DMA
-    jobs, parts = pl.pallas_call(
-        functools.partial(share_kernel, n_rep),
+    smem = pl.BlockSpec(memory_space=pltpu.SMEM)
+    jobs = n * LANES
+    stack, flag = pl.pallas_call(
+        functools.partial(newton_kernel, n_geo, n_rep),
         out_shape=[
-            jax.ShapeDtypeStruct((4, n_rep * n, LANES), F32),
-            jax.ShapeDtypeStruct((3, PART, tracts), F32),
+            jax.ShapeDtypeStruct((4, n_rep * PART, tracts), F32),
+            jax.ShapeDtypeStruct((1, 1), jnp.int32),
         ],
         in_specs=[vmem] * 9,
-        out_specs=[vmem] * 2,
+        out_specs=[vmem, smem],
         scratch_shapes=[
-            pltpu.VMEM((4 * n, LANES), F32),
-            pltpu.VMEM((n_rep, 4 * n, LANES), F32),
             pltpu.VMEM((3, n_rep * PART, tracts), F32),
+            pltpu.VMEM((n_rep * LANES, jobs), BF),
+            pltpu.VMEM((n_rep * LANES, jobs), F32),
+            pltpu.VMEM((6 * SUB, jobs), BF),
+            pltpu.VMEM((6 * SUB, n_rep * LANES), F32),
+            pltpu.VMEM((n_rep, 3 * SUB, LANES), F32),
+            pltpu.VMEM((n_rep, 3 * SUB, LANES), F32),
+            pltpu.VMEM((CAP * LANES, tracts), BF),
+            pltpu.VMEM((CAP * LANES, tracts), BF),
+            pltpu.VMEM((4 * PART, CAP * LANES), BF),
+            pltpu.VMEM((5, LANES, 1, LANES), F32),
+            pltpu.VMEM((5, LANES, 1, LANES), F32),
+            pltpu.VMEM((n_rep, 9 * PART, tracts), F32),
             dma((n_rep - 1,)),
             dma((n_rep - 1,)),
+            dma((5,)),
+            dma((5,)),
+            dma((2, n_rep - 1)),
+            dma((2, n_rep - 1)),
         ],
-        compiler_params=pltpu.CompilerParams(collective_id=0, has_side_effects=True),
-        name="share",
+        compiler_params=pltpu.CompilerParams(
+            collective_id=0, has_side_effects=True, vmem_limit_bytes=40 * 2**20
+        ),
+        name="newton",
     )(
         base.reshape(n, LANES),
         job_res.reshape(n, LANES),
@@ -463,36 +493,16 @@
         target_res,
         target_work,
     )
-    count = n_rep * n * LANES
     out = jax.ShapeDtypeStruct((cells, tracts), F32)
-    *fast, flag = pl.pallas_call(
-        functools.partial(newton_kernel, n_geo, n_rep),
-        out_shape=[out] * 4 + [jax.ShapeDtypeStruct((8, LANES), F32)],
-        in_specs=[vmem] * 2,
-        out_specs=[vmem] * 5,
-        scratch_shapes=[
-            pltpu.VMEM((LANES, count), BF),
-            pltpu.VMEM((LANES, count), F32),
-            pltpu.VMEM((8, LANES), F32),
-            pltpu.VMEM((6 * CAP, count), BF),
-            pltpu.VMEM((6 * CAP, LANES), F32),
-            pltpu.VMEM((CAP * LANES, tracts), BF),
-            pltpu.VMEM((CAP * LANES, tracts), BF),
-            pltpu.VMEM((4 * PART, CAP * LANES), BF),
-            pltpu.VMEM((5, LANES, 1, LANES), F32),
-            pltpu.VMEM((5, LANES, 1, LANES), F32),
-            pltpu.VMEM((n_rep, 9 * PART, tracts), F32),
-            dma((5,)),
-            dma((5,)),
-            dma((2, n_rep - 1)),
-            dma((2, n_rep - 1)),
-        ],
-        compiler_params=pltpu.CompilerParams(
-            collective_id=1, has_side_effects=True, vmem_limit_bytes=48 * 2**20
-        ),
-        name="newton",
-    )(jobs, parts)
-    return lax.cond(flag[0, 0] == 0.0, lambda: tuple(fast), lambda: tuple(general(*args)))
+
+    def fast():
+        return tuple(
+            pl.pallas_call(
+                hand_out, out_shape=[out] * 4, in_specs=[vmem], out_specs=[vmem] * 4, name="finish"
+            )(stack)
+        )
+
+    return lax.cond(flag[0, 0] == 0, fast, lambda: tuple(general(*args)))
 
 
 def solution(mesh):

time: 91.5 us -> 70.2 us (0.77)
  Pallas kernels: 81.7 us -> 68.5 us
  local copies, waits for them, and re-layouts: 7.64 us -> 0 us
    pallas_call x1, Pallas kernels: 8.44 us -> 0.66 us  [fast(): pl.pallas_call(hand_out, out_shape=[out] * 4, in_specs=[vmem], out_specs=...]
    unnamed x8 -> x0, local copies, waits for them, and re-layouts: 7.13 us -> none
    pallas_call x1, Pallas kernels: 73.2 us -> 67.8 us  [body(): pl.pallas_call(functools.partial(newton_kernel, n_geo, n_rep), out_shape=...]
where the time goes in v2:
time: 70.2 us; the launch traced here: 70 us
  Pallas kernels  68.5 us (98%)
  between operations  1.33 us (2%)
    pallas_call x1, Pallas kernels, body(): pl.pallas_call(functools.partial(newton_kernel, n_geo, n_rep), out_shape=...  67.8 us

profile of v2, /device:TPU:1, one launch (start us, length us, event | category | flops | bytes accessed | tf_op | source)
XLA Modules:
  0.0 70.0 jit_solution(9607188051653422106)
XLA Ops:
  0.6 67.8 %newton.1 = (f32[4,32,256]{2,1,0:T(8,128)S(1)}, s32[1,1]{1,0:T(1,128)}) custom-call(f32[16,128]{1,0:T(8,128)} %bitcast.153, s32[16,128]{1,0:T(8,128)} %bitcast.150, s32[16,128]{1,0:T(8,128)} %bitcast.151, s32[16,128]{1,0:T(8,128)} %bitcast.152, s32[1,128]{1,0:T(1,128)} %bitcast.154, f32[30,256]{1,0:T(8,128)} %lam_res.1, f32[30,256]{1,0:T(8,128)} %lam_work.1, ...), custom_call_target="tpu_custom_call" | custom-call | tf_op jit(solution)/shard_map/newton/pallas_call | solution.py:452
  69.1 0.9 %conditional.1 = ((f32[30,256]{1,0:T(8,128)}, f32[30,256]{1,0:T(8,128)}, f32[30,256]{1,0:T(8,128)}, f32[30,256]{1,0:T(8,128)})) conditional(s32[]{:T(128)} %bitcast.27, (s32[2048]{0:T(1024)}, s32[2048]{0:T(1024)}, f32[30,256]{1,0:T(8,128)}, s32[1,128,1]{1,2,0:T(1,128)}, f32[30,256]{1,0:T(8,128)}, /*index=5*/s32[2048]{0:T(1024)}, f32[2048]{0:T(1024)}, ...), branch_computations={%region_0.20_spmd, %region_20.21_spmd} | conditional | flops 25986052 | bytes 36274240 | solution.py:505
  69.4 0.7 finish.1

commit v3 on v2

--- a/solution.py
+++ b/solution.py
@@ -133,63 +133,70 @@
     parts = [wide[k, mine, :] for k in range(3)]
     pl.semaphore_wait(barrier, n_geo - 1 + n_rep - 1)
 
-    copies = []
-    for i in range(1, n_rep):
-        other = lax.rem(r + i, n_rep)
-        copy = pltpu.make_async_remote_copy(
-            src_ref=xsend.at[other],
-            dst_ref=xlist.at[r],
-            send_sem=list_send_sem.at[i - 1],
-            recv_sem=list_recv_sem.at[i - 1],
-            device_id=(g, other),
-            device_id_type=MESH,
-        )
-        copy.start()
-        copies.append(copy)
+    def swap(lo, hi, which):
+        copies = []
+        for i in range(1, n_rep):
+            other = lax.rem(r + i, n_rep)
+            copy = pltpu.make_async_remote_copy(
+                src_ref=xsend.at[other, pl.ds(lo, hi - lo)],
+                dst_ref=xlist.at[r, pl.ds(lo, hi - lo)],
+                send_sem=list_send_sem.at[which, i - 1],
+                recv_sem=list_recv_sem.at[which, i - 1],
+                device_id=(g, other),
+                device_id_type=MESH,
+            )
+            copy.start()
+            copies.append(copy)
+        return copies
+
+    lists_now = swap(0, 2 * SUB, 0)
+    lists_later = swap(2 * SUB, 3 * SUB, 1)
     xlist[r] = xsend[r]
-    for copy in copies:
+    for copy in lists_now:
         copy.wait()
-    merged = [jnp.zeros((CAP, LANES), F32)] * 3
-    offset = jnp.zeros((1, LANES), jnp.int32)
-    empty = jnp.zeros((CAP - SUB, LANES), F32)
-    for q in range(n_rep):
-        lists = [xlist[q, f * SUB : (f + 1) * SUB, :] for f in range(3)]
-        count = jnp.sum(jnp.where(lists[0] > 0.0, 1, 0), axis=0, keepdims=True)
-        lists = [jnp.concatenate([x, empty], axis=0) for x in lists]
-        if q:
-            for bit in range(6):
-                moved = (offset >> bit) & 1 == 1
-                width = 1 << bit
-                gap = jnp.zeros((width, LANES), F32)
-                lists = [
-                    jnp.where(moved, jnp.concatenate([gap, x[: CAP - width]], axis=0), x)
-                    for x in lists
-                ]
-        merged = [x + y for x, y in zip(merged, lists)]
-        offset = offset + count
-    crowded = jnp.logical_or(most > SUB, jnp.max(offset) > CAP)
-    u_g, work_g, home_g = merged
-    home_g = home_g.astype(jnp.int32)
-    cell_g = home_g >> 8
-    res_g = (home_g & 255).astype(F32)
+
+    counts = [
+        jnp.sum(jnp.where(xlist[q, 0:SUB, :] > 0.0, 1, 0), axis=0, keepdims=True)
+        for q in range(n_rep)
+    ]
+
+    def merge(field):
+        total = jnp.zeros((CAP, LANES), F32)
+        offset = jnp.zeros((1, LANES), jnp.int32)
+        for q in range(n_rep):
+            x = xlist[q, field * SUB : (field + 1) * SUB, :]
+            x = jnp.concatenate([x, jnp.zeros((CAP - SUB, LANES), F32)], axis=0)
+            if q:
+                for bit in range(6):
+                    width = 1 << bit
+                    gap = jnp.zeros((width, LANES), F32)
+                    down = jnp.concatenate([gap, x[: CAP - width]], axis=0)
+                    x = jnp.where((offset >> bit) & 1 == 1, down, x)
+            total = total + x
+            offset = offset + counts[q]
+        return total
+
+    crowded = jnp.logical_or(
+        most > SUB, jnp.max(counts[0] + counts[1] + counts[2] + counts[3]) > CAP
+    )
 
     pad = jnp.zeros((LANES - 2 * CAP, LANES), F32)
 
     def launch(k, first, second):
         whole = jnp.concatenate([first, second, pad], axis=0)
-        send[k] = jnp.transpose(whole).reshape(LANES, 1, LANES)
+        send[k] = jnp.transpose(whole)
 
         each_peer(
             lambda peer: pltpu.make_async_remote_copy(
-                src_ref=send.at[k, peer],
-                dst_ref=recv.at[k, g],
+                src_ref=send.at[k, pl.ds(peer, 1)],
+                dst_ref=recv.at[k, pl.ds(g, 1)],
                 send_sem=send_sem.at[k],
                 recv_sem=recv_sem.at[k],
                 device_id=(peer, r),
                 device_id_type=MESH,
             ).start()
         )
-        recv[k, g] = send[k, g]
+        recv[k, pl.ds(g, 1), :] = send[k, pl.ds(g, 1), :]
 
     def everything(k):
         return pltpu.make_async_remote_copy(
@@ -203,65 +210,74 @@
 
     def arrive(k):
         everything(k).wait_recv()
-        return jnp.transpose(recv[k].reshape(LANES, LANES))
+        return jnp.transpose(recv[k])
 
     def over(x):
         x = x.astype(F32)
         return jnp.transpose(jnp.concatenate([x, jnp.zeros((LANES - CAP, LANES), F32)], axis=0))
 
-    tracts = lax.broadcasted_iota(jnp.int32, (LANES, 256), 1).astype(F32)
+    tracts = lax.broadcasted_iota(jnp.int32, (LANES, LANES), 1).astype(F32)
 
     def columns(oht, numbers):
         for k in range(CAP):
             hot = jnp.where(numbers[:, k : k + 1] == tracts, 1.0, 0.0)
             oht[k * LANES : (k + 1) * LANES, :] = hot.astype(BF)
 
-    lines = lax.broadcasted_iota(jnp.int32, (PART, LANES), 0)
-
-    def scatter(values, cell, oht):
+    lines = lax.broadcasted_iota(jnp.int32, (2 * PART, LANES), 0)
+
+    def line_of(index):
+        return (index >> 8) + PART * ((index >> 7) & 1)
+
+    def scatter(values, line, oht):
         pieces = [piece for value in values for piece in split(value)]
+        high = 2 * PART
         for k in range(CAP):
-            mine = cell[k : k + 1, :] == lines
+            mine = line[k : k + 1, :] == lines
             stack = [jnp.where(mine, piece[k : k + 1, :], 0.0) for piece in pieces]
-            left[0 : PART * len(pieces), k * LANES : (k + 1) * LANES] = jnp.concatenate(
+            left[0 : high * len(pieces), k * LANES : (k + 1) * LANES] = jnp.concatenate(
                 stack, axis=0
             ).astype(BF)
-        out = jnp.dot(left[0 : PART * len(pieces), :], oht[...], preferred_element_type=F32)
-        return [
-            out[2 * v * PART : (2 * v + 1) * PART] + out[(2 * v + 1) * PART : (2 * v + 2) * PART]
+        out = jnp.dot(left[0 : high * len(pieces), :], oht[...], preferred_element_type=F32)
+        sums = [
+            out[2 * v * high : (2 * v + 1) * high] + out[(2 * v + 1) * high : (2 * v + 2) * high]
             for v in range(len(values))
         ]
-
-    launch(0, u_g, work_g)
-    columns(oht_r, over(res_g))
+        return [jnp.concatenate([x[:PART], x[PART:]], axis=1) for x in sums]
+
+    launch(0, merge(0), merge(1))
+    for copy in lists_later:
+        copy.wait()
+    home_g = merge(2).astype(jnp.int32)
+    line_g = line_of(home_g)
+    columns(oht_r, over(home_g & 127))
 
     flat = arrive(0)
     u_o = flat[0:CAP]
     work_o = flat[CAP : 2 * CAP].astype(jnp.int32)
-    cell_o = work_o >> 8
-    columns(oht_w, over(work_o & 255))
+    line_o = line_of(work_o)
+    columns(oht_w, over(work_o & 127))
     w_o = u_o * gather(jnp.exp(parts[0]), work_o, PART)
-    [sum_w] = scatter([w_o], cell_o, oht_w)
+    [sum_w] = scatter([w_o], line_o, oht_w)
     diag_w = sum_w + RIDGE
     b0 = parts[2] - sum_w
     launch(1, w_o, gather(b0, work_o, PART))
 
     flat = arrive(1)
     w_g = flat[0:CAP]
-    sum_r, bb0 = scatter([w_g, w_g * flat[CAP : 2 * CAP]], cell_g, oht_r)
+    sum_r, bb0 = scatter([w_g, w_g * flat[CAP : 2 * CAP]], line_g, oht_r)
     diag_r = sum_r + RIDGE
     a0 = parts[1] - sum_r
     a1 = diag_r * a0 + bb0
     launch(2, w_g * gather(a0, home_g, PART), w_g * gather(a1, home_g, PART))
 
     flat = arrive(2)
-    ba0, ba1 = scatter([flat[0:CAP], flat[CAP : 2 * CAP]], cell_o, oht_w)
+    ba0, ba1 = scatter([flat[0:CAP], flat[CAP : 2 * CAP]], line_o, oht_w)
     b1 = diag_w * b0 + ba0
     b2 = diag_w * b1 + ba1
     launch(3, w_o * gather(b1, work_o, PART), w_o * gather(b2, work_o, PART))
 
     flat = arrive(3)
-    bb1, bb2 = scatter([flat[0:CAP], flat[CAP : 2 * CAP]], cell_g, oht_r)
+    bb1, bb2 = scatter([flat[0:CAP], flat[CAP : 2 * CAP]], line_g, oht_r)
     a2 = diag_r * a1 + bb1
     a3 = diag_r * a2 + bb2
 
@@ -313,7 +329,7 @@
     first = across(0, early, 0)
 
     flat = arrive(4)
-    [ba2] = scatter([flat[0:CAP]], cell_o, oht_w)
+    [ba2] = scatter([flat[0:CAP]], line_o, oht_w)
     b3 = diag_w * b2 + ba2
     xbuf[r, early : early + PART, :] = b3
     xbuf[r, early + PART : early + 2 * PART, :] = jnp.broadcast_to(
@@ -465,14 +481,14 @@
             pltpu.VMEM((6 * SUB, n_rep * LANES), F32),
             pltpu.VMEM((n_rep, 3 * SUB, LANES), F32),
             pltpu.VMEM((n_rep, 3 * SUB, LANES), F32),
-            pltpu.VMEM((CAP * LANES, tracts), BF),
-            pltpu.VMEM((CAP * LANES, tracts), BF),
-            pltpu.VMEM((4 * PART, CAP * LANES), BF),
-            pltpu.VMEM((5, LANES, 1, LANES), F32),
-            pltpu.VMEM((5, LANES, 1, LANES), F32),
+            pltpu.VMEM((CAP * LANES, LANES), BF),
+            pltpu.VMEM((CAP * LANES, LANES), BF),
+            pltpu.VMEM((8 * PART, CAP * LANES), BF),
+            pltpu.VMEM((5, LANES, LANES), F32),
+            pltpu.VMEM((5, LANES, LANES), F32),
             pltpu.VMEM((n_rep, 9 * PART, tracts), F32),
-            dma((n_rep - 1,)),
-            dma((n_rep - 1,)),
+            dma((2, n_rep - 1)),
+            dma((2, n_rep - 1)),
             dma((5,)),
             dma((5,)),
             dma((2, n_rep - 1)),

time: 70.2 us -> 67.6 us (0.963)
  Pallas kernels: 68.5 us -> 65.9 us
    pallas_call x1, Pallas kernels: 67.8 us -> 65.2 us  [body(): pl.pallas_call(functools.partial(newton_kernel, n_geo, n_rep), out_shape=...]
where the time goes in v3:
time: 67.6 us; the launch traced here: 67.4 us
  Pallas kernels  65.9 us (97%)
  between operations  1.33 us (2%)
    pallas_call x1, Pallas kernels, body(): pl.pallas_call(functools.partial(newton_kernel, n_geo, n_rep), out_shape=...  65.2 us

profile of v3, /device:TPU:1, one launch (start us, length us, event | category | flops | bytes accessed | tf_op | source)
XLA Modules:
  0.0 67.4 jit_solution(2522521396358500232)
XLA Ops:
  0.6 65.2 %newton.1 = (f32[4,32,256]{2,1,0:T(8,128)S(1)}, s32[1,1]{1,0:T(1,128)}) custom-call(f32[16,128]{1,0:T(8,128)} %bitcast.153, s32[16,128]{1,0:T(8,128)} %bitcast.150, s32[16,128]{1,0:T(8,128)} %bitcast.151, s32[16,128]{1,0:T(8,128)} %bitcast.152, s32[1,128]{1,0:T(1,128)} %bitcast.154, f32[30,256]{1,0:T(8,128)} %lam_res.1, f32[30,256]{1,0:T(8,128)} %lam_work.1, ...), custom_call_target="tpu_custom_call" | custom-call | tf_op jit(solution)/shard_map/newton/pallas_call | solution.py:468
  66.5 0.9 %conditional.1 = ((f32[30,256]{1,0:T(8,128)}, f32[30,256]{1,0:T(8,128)}, f32[30,256]{1,0:T(8,128)}, f32[30,256]{1,0:T(8,128)})) conditional(s32[]{:T(128)} %bitcast.27, (s32[2048]{0:T(1024)}, s32[2048]{0:T(1024)}, f32[30,256]{1,0:T(8,128)}, s32[1,128,1]{1,2,0:T(1,128)}, f32[30,256]{1,0:T(8,128)}, /*index=5*/s32[2048]{0:T(1024)}, f32[2048]{0:T(1024)}, ...), branch_computations={%region_0.20_spmd, %region_20.21_spmd} | conditional | flops 25986052 | bytes 36274240 | solution.py:521
  66.8 0.7 finish.1

commit v4 on v3

--- a/solution.py
+++ b/solution.py
@@ -39,12 +39,29 @@
 
 
 def newton_kernel(
-    n_geo, n_rep, base, res, slot, cell, needed, lam_res, lam_work, t_res, t_work, o_all, o_flag,
-    wide, ohp, pre, fields, place, xsend, xlist, oht_r, oht_w, left, send, recv, xbuf,
+    n_geo, n_rep, *refs
+):
+    operands, (o_all, o_flag), held = refs[:9], refs[9:11], refs[11:20]
+    base, res, slot, cell, needed, lam_res, lam_work, t_res, t_work = held
+    run_newton(
+        n_geo, n_rep, operands, held, base, res, slot, cell, needed, lam_res, lam_work, t_res,
+        t_work, o_all, o_flag, *refs[20:]
+    )
+
+
+def run_newton(
+    n_geo, n_rep, operands, held, base, res, slot, cell, needed, lam_res, lam_work, t_res, t_work,
+    o_all, o_flag, held_sem, wide, ohp, pre, fields, place, xsend, xlist, oht_r, oht_w, left, send, recv, xbuf,
     list_send_sem, list_recv_sem, send_sem, recv_sem, xsend_sem, xrecv_sem,
 ):
     g, r = lax.axis_index("geo"), lax.axis_index("rep")
     barrier = pltpu.get_barrier_semaphore()
+
+    loads = []
+    for k, (source, target) in enumerate(zip(operands, held)):
+        load = pltpu.make_async_copy(source, target, held_sem.at[k])
+        load.start()
+        loads.append(load)
 
     depth = n_geo // 16
     z, y, core = g // 16, lax.rem(g // 2, 8), lax.rem(g, 2)
@@ -73,6 +90,8 @@
             barrier, inc=1, device_id=(g, lax.rem(r + i, n_rep)), device_id_type=MESH
         )
 
+    for load in loads:
+        load.wait()
     cells = lam_res.shape[0]
     c = cell[...]
     s = slot[...]
@@ -133,9 +152,11 @@
     parts = [wide[k, mine, :] for k in range(3)]
     pl.semaphore_wait(barrier, n_geo - 1 + n_rep - 1)
 
+    around = sorted(range(1, n_rep), key=lambda i: -min(i, n_rep - i))
+
     def swap(lo, hi, which):
         copies = []
-        for i in range(1, n_rep):
+        for i in around:
             other = lax.rem(r + i, n_rep)
             copy = pltpu.make_async_remote_copy(
                 src_ref=xsend.at[other, pl.ds(lo, hi - lo)],
@@ -153,7 +174,7 @@
     lists_later = swap(2 * SUB, 3 * SUB, 1)
     xlist[r] = xsend[r]
     for copy in lists_now:
-        copy.wait()
+        copy.wait_recv()
 
     counts = [
         jnp.sum(jnp.where(xlist[q, 0:SUB, :] > 0.0, 1, 0), axis=0, keepdims=True)
@@ -176,9 +197,8 @@
             offset = offset + counts[q]
         return total
 
-    crowded = jnp.logical_or(
-        most > SUB, jnp.max(counts[0] + counts[1] + counts[2] + counts[3]) > CAP
-    )
+    total = sum(counts[1:], counts[0])
+    crowded = jnp.where(jnp.logical_or(most > SUB, total > CAP), 1.0, 0.0)
 
     pad = jnp.zeros((LANES - 2 * CAP, LANES), F32)
 
@@ -246,7 +266,7 @@
 
     launch(0, merge(0), merge(1))
     for copy in lists_later:
-        copy.wait()
+        copy.wait_recv()
     home_g = merge(2).astype(jnp.int32)
     line_g = line_of(home_g)
     columns(oht_r, over(home_g & 127))
@@ -285,8 +305,9 @@
         x = x[:, 0:LANES] + x[:, LANES : 2 * LANES]
         return jnp.sum(x, axis=0, keepdims=True)
 
-    steep = jnp.maximum(jnp.max(sum_r), jnp.max(sum_w))
-    bad = jnp.where(jnp.logical_or(steep > STEEP, crowded), 1.0, 0.0)
+    steep = jnp.maximum(sum_r, sum_w)
+    steep = jnp.max(jnp.maximum(steep[:, :LANES], steep[:, LANES:]), axis=0, keepdims=True)
+    bad = jnp.where(steep > STEEP, 1.0, crowded)
     table = jnp.concatenate(
         [
             line(a0 * a0 + b0 * b0),
@@ -295,7 +316,7 @@
             line(a1 * a2 + b1 * b2),
             line(a2 * a2 + b2 * b2),
             line(a2 * (a3 + bb2) + diag_w * b2 * b2),
-            jnp.full((1, LANES), bad, F32),
+            bad,
             jnp.zeros((1, LANES), F32),
         ],
         axis=0,
@@ -313,7 +334,7 @@
 
     def across(lo, hi, which):
         copies = []
-        for i in range(1, n_rep):
+        for i in around:
             copy = pltpu.make_async_remote_copy(
                 src_ref=xbuf.at[r, pl.ds(lo, hi - lo)],
                 dst_ref=xbuf.at[r, pl.ds(lo, hi - lo)],
@@ -337,9 +358,7 @@
     )
     last = across(early, early + 2 * PART, 1)
     for copy in first + last:
-        copy.wait()
-    for k in range(5):
-        everything(k).wait_send()
+        copy.wait_recv()
 
     sums = xbuf[0, early + PART : early + 2 * PART, :]
     for q in range(1, n_rep):
@@ -379,6 +398,10 @@
             k = [xbuf[q, (4 * side + i) * PART : (4 * side + i + 1) * PART, :] for i in range(4)]
             o_all[side, lo : lo + PART, :] = xc[0] * k[0] + xc[1] * k[1] + xc[2] * k[2]
             o_all[2 + side, lo : lo + PART, :] = k[0] + rc[1] * k[1] + rc[2] * k[2] + rc[3] * k[3]
+    for copy in lists_now + lists_later + first + last:
+        copy.wait_send()
+    for k in range(5):
+        everything(k).wait_send()
 
 
 def hand_out(stack, *outs):
@@ -463,6 +486,8 @@
     cells, tracts = lam_res.shape
     vmem = pl.BlockSpec(memory_space=pltpu.VMEM)
     dma = pltpu.SemaphoreType.DMA
+    operands = [x.reshape(n, LANES) for x in (base, job_res, job_slot, job_cell)]
+    operands += [needed.reshape(1, LANES), lam_res, lam_work, target_res, target_work]
     smem = pl.BlockSpec(memory_space=pltpu.SMEM)
     jobs = n * LANES
     stack, flag = pl.pallas_call(
@@ -471,9 +496,11 @@
             jax.ShapeDtypeStruct((4, n_rep * PART, tracts), F32),
             jax.ShapeDtypeStruct((1, 1), jnp.int32),
         ],
-        in_specs=[vmem] * 9,
+        in_specs=[pl.BlockSpec(memory_space=pltpu.HBM)] * 9,
         out_specs=[vmem, smem],
-        scratch_shapes=[
+        scratch_shapes=[pltpu.VMEM(x.shape, x.dtype) for x in operands]
+        + [
+            dma((len(operands),)),
             pltpu.VMEM((3, n_rep * PART, tracts), F32),
             pltpu.VMEM((n_rep * LANES, jobs), BF),
             pltpu.VMEM((n_rep * LANES, jobs), F32),
@@ -498,17 +525,7 @@
             collective_id=0, has_side_effects=True, vmem_limit_bytes=40 * 2**20
         ),
         name="newton",
-    )(
-        base.reshape(n, LANES),
-        job_res.reshape(n, LANES),
-        job_slot.reshape(n, LANES),
-        job_cell.reshape(n, LANES),
-        needed.reshape(1, LANES),
-        lam_res,
-        lam_work,
-        target_res,
-        target_work,
-    )
+    )(*operands)
     out = jax.ShapeDtypeStruct((cells, tracts), F32)
 
     def fast():

time: 67.6 us -> 66.8 us (0.988)
  Pallas kernels: 65.9 us -> 65.1 us
    pallas_call x1, Pallas kernels: 65.2 us -> 64.4 us  [body(): pl.pallas_call(functools.partial(newton_kernel, n_geo, n_rep), out_shape=...]
where the time goes in v4:
time: 66.8 us; the launch traced here: 66.6 us
  Pallas kernels  65.1 us (97%)
  between operations  1.33 us (2%)
    pallas_call x1, Pallas kernels, body(): pl.pallas_call(functools.partial(newton_kernel, n_geo, n_rep), out_shape=...  64.4 us

profile of v4, /device:TPU:1, one launch (start us, length us, event | category | flops | bytes accessed | tf_op | source)
XLA Modules:
  0.0 66.6 jit_solution(11943399134067189899)
XLA Ops:
  0.6 64.4 %newton.1 = (f32[4,32,256]{2,1,0:T(8,128)S(1)}, s32[1,1]{1,0:T(1,128)}) custom-call(f32[16,128]{1,0:T(8,128)} %bitcast.153, s32[16,128]{1,0:T(8,128)} %bitcast.150, s32[16,128]{1,0:T(8,128)} %bitcast.151, s32[16,128]{1,0:T(8,128)} %bitcast.152, s32[1,128]{1,0:T(1,128)} %bitcast.154, f32[30,256]{1,0:T(8,128)} %refs_5_.1, f32[30,256]{1,0:T(8,128)} %refs_6_.1, ...), custom_call_target="tpu_custom_call" | custom-call | tf_op jit(solution)/shard_map/newton/pallas_call | solution.py:493
  65.7 0.9 %conditional.1 = ((f32[30,256]{1,0:T(8,128)}, f32[30,256]{1,0:T(8,128)}, f32[30,256]{1,0:T(8,128)}, f32[30,256]{1,0:T(8,128)})) conditional(s32[]{:T(128)} %bitcast.27, (s32[2048]{0:T(1024)}, s32[2048]{0:T(1024)}, f32[30,256]{1,0:T(8,128)}, s32[1,128,1]{1,2,0:T(1,128)}, f32[30,256]{1,0:T(8,128)}, /*index=5*/s32[2048]{0:T(1024)}, f32[2048]{0:T(1024)}, ...), branch_computations={%region_0.20_spmd, %region_20.21_spmd} | conditional | flops 25986052 | bytes 36274240 | solution.py:538
  66.0 0.7 finish.1
